TPU v7x, 512 devices: a whole 4x4x16 slice. The times are simulated.
512 devices in a mesh: pair: 64 (over x, z), virt: 8 (over y, core).
Axes of the slice: x: 4, y: 4, z: 16, core: 2. Of those that a mesh axis runs over, the one named last changes fastest.
Arguments:
- amplitudes: bfloat16 [2, 64, 1024, 1024], P(None, 'pair', None, 'virt'), may hold values from -8.5 to 8.5, as said below
- w_ovvo: bfloat16 [64, 1024, 1024], P('pair', 'virt'), may hold values from -0.09375 to 0.09375
- occ_irreps: int32 [8], replicated, may hold values from 0 to 7
- vir_irreps: int32 [1024], replicated, may hold values from 0 to 7, as said below
Outputs:
- sigma_cycle: bfloat16 [2, 64, 1024, 1024], P(None, 'pair', None, 'virt')
Inputs may be any that keep to these rules, and one draw needn't show every extreme that they name: amplitudes[x, i*8+j, a, b] equals amplitudes[x, j*8+i, b, a] exactly. `vir_irreps`: non-decreasing along the orbitals, so each irrep is one contiguous block; the first entry is 0 and the last 7.
All inputs are finite; a program needn't handle non-finite values.
Results may differ from a plain program's by a relative error of at most 0.017.
Values may be sent and summed in bfloat16 or wider, within the bound.
A program may use at most 64 MiB of HBM per device.

v0:
```python
import math

import jax
import jax.numpy as jnp
from jax import lax
from jax.sharding import PartitionSpec as P


def swapped(block, axis, stride):
    count = lax.axis_size(axis)
    route = []
    for low in range(count):
        high = low | 1 << stride
        if high != low and high < count:
            route += [(low, high), (high, low)]
    return lax.ppermute(block, axis, route)


def bit_of(position, level):
    return position // 2**level % 2


def shards(amplitudes, w_ovvo, occ_irreps, vir_irreps):
    own_tile = amplitudes[:, 0]
    devices = lax.axis_size("pair")
    tiles_side = math.isqrt(devices)
    bit_count = tiles_side.bit_length() - 1
    position = lax.axis_index("pair")
    spread = lax.all_to_all(own_tile[None], "pair", split_axis=2, concat_axis=0, tiled=True)
    shape_rest = spread.shape[1:]
    spread = spread.reshape((tiles_side, tiles_side) + shape_rest)
    spread = jnp.swapaxes(spread, 0, 1).reshape((devices,) + shape_rest)
    mirrored = lax.all_to_all(spread, "pair", split_axis=0, concat_axis=2, tiled=True)[0]
    cycle_tile = (2.0 * own_tile.astype(jnp.float32) - mirrored.astype(jnp.float32)).astype(
        jnp.bfloat16
    )
    cycle_stack = cycle_tile[None]
    for level in range(bit_count):
        partner = swapped(cycle_stack, "pair", level)
        lower_half = bit_of(position, level) == 0
        cycle_stack = jnp.where(
            lower_half,
            jnp.concatenate([cycle_stack, partner], axis=0),
            jnp.concatenate([partner, cycle_stack], axis=0),
        )
    weight_stack = w_ovvo
    for level in range(bit_count):
        partner = swapped(weight_stack, "pair", level + bit_count)
        lower_half = bit_of(position, level + bit_count) == 0
        weight_stack = jnp.where(
            lower_half,
            jnp.concatenate([weight_stack, partner], axis=0),
            jnp.concatenate([partner, weight_stack], axis=0),
        )
    partial_value = jnp.einsum(
        "kxac,kcb->xab", cycle_stack, weight_stack, preferred_element_type=jnp.float32
    )
    summed = lax.psum_scatter(
        partial_value.astype(jnp.bfloat16), "virt", scatter_dimension=2, tiled=True
    ).astype(jnp.float32)
    width_local = summed.shape[2]
    occ_order = jnp.arange(occ_irreps.shape[0], dtype=jnp.int32)
    left_irrep = jnp.sum(jnp.where(occ_order == position // tiles_side, occ_irreps, 0))
    right_irrep = jnp.sum(jnp.where(occ_order == position % tiles_side, occ_irreps, 0))
    column_irreps = lax.dynamic_slice_in_dim(
        vir_irreps, lax.axis_index("virt") * width_local, width_local
    )
    target = jnp.bitwise_xor(left_irrep, right_irrep)
    allowed = jnp.bitwise_xor(vir_irreps[:, None], column_irreps[None, :]) == target
    result = jnp.where(allowed[None], summed, 0.0).astype(jnp.bfloat16)
    return result[:, None]


def solution(mesh):
    in_specs = (P(None, "pair", None, "virt"), P("pair", "virt", None), P(), P())
    out_specs = P(None, "pair", None, "virt")
    return jax.shard_map(shards, mesh=mesh, in_specs=in_specs, out_specs=out_specs, check_vma=False)
```

profile of v0, /device:TPU:6, one launch (start us, length us, event | category | flops | bytes accessed | tf_op | source)
XLA Modules:
  0.0 459.9 jit_solution(16035871739687931786)
XLA Ops:
  6.5 0.0 reduce-scatter.4.cloned.1.call-start
  6.5 1.6 copy.24
  8.1 50.3 %all_to_all.24 = bf16[1,2,1024,128]{3,1,0,2:T(2,128)(2,1)S(1)} all-to-all(bf16[1,2,1024,128]{3,1,0,2:T(2,128)(2,1)S(1)} %bitcast.39), channel_id=1, replica_groups=mesh['pair'=64,'virt'=8] {'pair'}, dimensions={2} | all-to-all | bytes 1048576 | tf_op jit(solution)/shard_map/all_to_all | solution.py:29
  58.4 0.1 copy.9
  58.5 37.3 %all_to_all.25 = bf16[64,2,16,128]{3,2,1,0:T(8,128)(2,1)S(1)} all-to-all(bf16[64,2,16,128]{3,2,1,0:T(8,128)(2,1)S(1)} %bitcast.37), channel_id=1, replica_groups=mesh['pair'=64,'virt'=8] {'pair'}, dimensions={0} | all-to-all | bytes 1048576 | tf_op jit(solution)/shard_map/all_to_all | solution.py:33
  95.7 0.0 copy-start
  95.7 0.1 convert_bitcast_fusion
  95.9 0.5 copy.10
  96.4 0.3 copy-done
  96.8 0.7 subtract_convert_fusion
  97.5 3.3 collective-permute-start
  100.9 11.1 %collective-permute-done = bf16[1,2,1024,128]{3,1,0,2:T(2,128)(2,1)S(1)} collective-permute-done((bf16[1,2,1024,128]{3,1,0,2:T(2,128)(2,1)S(1)}, bf16[1,2,1024,128]{3,1,0,2:T(2,128)(2,1)S(1)}, u32[]{:S(2)}, u32[]{:S(2)}) %collective-permute-start) | collective-permute-done | bytes 524320 | tf_op jit(solution)/shard_map/ppermute | solution.py:16
  112.0 2.1 broadcast_select_fusion.2
  114.1 2.3 collective-permute-start.1
  116.4 0.0 copy-start.1
  116.4 45.9 %collective-permute-done.1 = bf16[2,2,1024,128]{3,1,0,2:T(2,128)(2,1)} collective-permute-done((bf16[2,2,1024,128]{3,1,0,2:T(2,128)(2,1)S(1)}, bf16[2,2,1024,128]{3,1,0,2:T(2,128)(2,1)}, u32[]{:S(2)}, u32[]{:S(2)}) %collective-permute-start.1) | collective-permute-done | bytes 1048608 | tf_op jit(solution)/shard_map/ppermute | solution.py:16
  162.3 5.7 %broadcast_select_fusion.1 = bf16[4,2,1024,128]{3,1,0,2:T(2,128)(2,1)S(1)} fusion(pred[]{:T(512)S(6)} %eq.55, bf16[2,2,1024,128]{3,1,0,2:T(2,128)(2,1)} %collective-permute-done.1, bf16[2,2,1024,128]{3,1,0,2:T(2,128)(2,1)S(1)} %broadcast_select_fusion.2), kind=kLoop, calls=%fused_computation.4 | loop fusion | flops 3145728 | bytes 4194305 | tf_op jit(solution)/shard_map/jit(_where)/select_n | solution.py:41
  168.1 3.6 collective-permute-start.2
  171.7 0.0 copy-done.1
  171.7 4.7 %collective-permute-start.3 = (bf16[1,128,1024]{2,1,0:T(8,128)(2,1)S(1)}, bf16[1,128,1024]{2,1,0:T(8,128)(2,1)S(1)}, u32[]{:S(2)}, u32[]{:S(2)}) collective-permute-start(bf16[1,128,1024]{2,1,0:T(8,128)(2,1)S(1)} %copy-done.1), channel_id=1, source_target_pairs={{0,64},{64,0},{8,72},{72,8},{16,80},{80,16},{24,88},{88,24},{32,96... | collective-permute-start | bytes 786440 | tf_op jit(solution)/shard_map/ppermute | solution.py:16
  176.4 60.7 %collective-permute-done.3 = bf16[1,128,1024]{2,1,0:T(8,128)(2,1)S(1)} collective-permute-done((bf16[1,128,1024]{2,1,0:T(8,128)(2,1)S(1)}, bf16[1,128,1024]{2,1,0:T(8,128)(2,1)S(1)}, u32[]{:S(2)}, u32[]{:S(2)}) %collective-permute-start.3) | collective-permute-done | bytes 262176 | tf_op jit(solution)/shard_map/ppermute | solution.py:16
  237.1 0.1 maximum_select_fusion.2
  237.2 3.0 collective-permute-start.4
  240.3 11.6 %collective-permute-done.4 = bf16[2,128,1024]{2,1,0:T(8,128)(2,1)S(1)} collective-permute-done((bf16[2,128,1024]{2,1,0:T(8,128)(2,1)S(1)}, bf16[2,128,1024]{2,1,0:T(8,128)(2,1)S(1)}, u32[]{:S(2)}, u32[]{:S(2)}) %collective-permute-start.4) | collective-permute-done | bytes 524320 | tf_op jit(solution)/shard_map/ppermute | solution.py:16
  251.9 0.2 maximum_select_fusion.1
  252.1 4.0 collective-permute-start.5
  256.1 120.1 %collective-permute-done.2 = bf16[4,2,1024,128]{3,1,0,2:T(2,128)(2,1)} collective-permute-done((bf16[4,2,1024,128]{3,1,0,2:T(2,128)(2,1)S(1)}, bf16[4,2,1024,128]{3,1,0,2:T(2,128)(2,1)}, u32[]{:S(2)}, u32[]{:S(2)}) %collective-permute-start.2) | collective-permute-done | bytes 2097184 | tf_op jit(solution)/shard_map/ppermute | solution.py:16
  376.2 10.5 %broadcast_select_fusion = bf16[8,2,1024,128]{3,1,0,2:T(2,128)(2,1)S(1)} fusion(pred[]{:T(512)S(6)} %eq.54, bf16[4,2,1024,128]{3,1,0,2:T(2,128)(2,1)} %collective-permute-done.2, bf16[4,2,1024,128]{3,1,0,2:T(2,128)(2,1)S(1)} %broadcast_select_fusion.1), kind=kLoop, calls=%fused_computation.1 | loop fusion | flops 6291456 | bytes 8388609 | tf_op jit(solution)/shard_map/jit(_where)/select_n | solution.py:41
  386.7 0.0 collective-permute-done.5
  386.7 6.2 %bitcast_convert_fusion = bf16[2,1024,1024]{2,1,0:T(8,128)(2,1)} fusion(bf16[8,2,1024,128]{3,1,0,2:T(2,128)(2,1)S(1)} %broadcast_select_fusion, bf16[4,128,1024]{2,1,0:T(8,128)(2,1)S(1)} %collective-permute-done.5, bf16[4,128,1024]{2,1,0:T(8,128)(2,1)S(1)} %maximum_select_fusion.1, pred[]{:T(512)S(6)} %eq.57), kind=kOutput, calls=%fused_computation | convolution fusion | flops 4300210176 | bytes 10485761 | tf_op jit(solution)/shard_map/kxac,kcb->xab/dot_general | solution.py:55
  392.9 11.3 %copy.14 = bf16[2,1024,1024]{1,0,2:T(2,128)(2,1)} copy(bf16[2,1024,1024]{2,1,0:T(8,128)(2,1)} %bitcast_convert_fusion) | data formatting | bytes 8388608
  404.2 5.5 %copy.16 = bf16[128,8,2,1024]{3,1,2,0:T(8,128)(2,1)} copy(bf16[128,8,2,1024]{3,2,1,0:T(2,128)(2,1)} %bitcast.34) | data formatting | bytes 8388608
  409.7 0.0 copy-start.3
  409.7 0.0 copy-start.2
  409.7 0.0 reduce-scatter.4.cloned.1.call-update
  409.8 0.6 copy-done.3
  410.4 0.7 fusion.14
  412.3 0.0 copy-done.2
  412.3 0.1 dynamic_slice.3
  412.4 0.2 xor_compare_fusion
  412.6 37.5 %reduce-scatter.4.cloned.1.call-done = bf16[128,2048]{1,0:T(8,128)(2,1)} async-done(((bf16[1024,2048]{1,0:T(8,128)(2,1)}), bf16[128,2048]{1,0:T(8,128)(2,1)}) %reduce-scatter.4.cloned.1.call-update) | async-done | bytes 524304
  450.1 1.4 reshape.76
  451.6 0.5 copy.15
  452.1 0.9 fusion.12
Async XLA Ops:
  6.5 443.6 %reduce-scatter.4.cloned.1.call-start = ((), (), s32[]{:S(2)}) async-start(), calls=%async_computation.3 | async-start | bytes 4718592
  95.7 1.0 copy-start
  97.5 14.5 %collective-permute-start = (bf16[1,2,1024,128]{3,1,0,2:T(2,128)(2,1)S(1)}, bf16[1,2,1024,128]{3,1,0,2:T(2,128)(2,1)S(1)}, u32[]{:S(2)}, u32[]{:S(2)}) collective-permute-start(bf16[1,2,1024,128]{3,1,0,2:T(2,128)(2,1)S(1)} %subtract_convert_fusion), channel_id=1, source_target_pairs={{0,8},{8,0},{16,24},{24,16},{32,40},{40,32},{48,56},{56,48},{64,72... | collective-permute-start | bytes 1572872 | tf_op jit(solution)/shard_map/ppermute | solution.py:16
  114.1 48.3 %collective-permute-start.1 = (bf16[2,2,1024,128]{3,1,0,2:T(2,128)(2,1)S(1)}, bf16[2,2,1024,128]{3,1,0,2:T(2,128)(2,1)}, u32[]{:S(2)}, u32[]{:S(2)}) collective-permute-start(bf16[2,2,1024,128]{3,1,0,2:T(2,128)(2,1)S(1)} %broadcast_select_fusion.2), channel_id=1, source_target_pairs={{0,16},{16,0},{8,24},{24,8},{32,48},{48,32},{40,56},{56,40},{64,80... | collective-permute-start | bytes 3145736 | tf_op jit(solution)/shard_map/ppermute | solution.py:16
  116.4 55.3 %copy-start.1 = (bf16[1,128,1024]{2,1,0:T(8,128)(2,1)S(1)}, bf16[1,128,1024]{2,1,0:T(8,128)(2,1)}, u32[]{:S(2)}) copy-start(bf16[1,128,1024]{2,1,0:T(8,128)(2,1)} %param.5) | copy-start | bytes 786436
  168.1 208.1 %collective-permute-start.2 = (bf16[4,2,1024,128]{3,1,0,2:T(2,128)(2,1)S(1)}, bf16[4,2,1024,128]{3,1,0,2:T(2,128)(2,1)}, u32[]{:S(2)}, u32[]{:S(2)}) collective-permute-start(bf16[4,2,1024,128]{3,1,0,2:T(2,128)(2,1)S(1)} %broadcast_select_fusion.1), channel_id=1, source_target_pairs={{0,32},{32,0},{8,40},{40,8},{16,48},{48,16},{24,56},{56,24},{64,96... | collective-permute-start | bytes 6291464 | tf_op jit(solution)/shard_map/ppermute | solution.py:16
  171.7 65.4 %collective-permute-start.3 = (bf16[1,128,1024]{2,1,0:T(8,128)(2,1)S(1)}, bf16[1,128,1024]{2,1,0:T(8,128)(2,1)S(1)}, u32[]{:S(2)}, u32[]{:S(2)}) collective-permute-start(bf16[1,128,1024]{2,1,0:T(8,128)(2,1)S(1)} %copy-done.1), channel_id=1, source_target_pairs={{0,64},{64,0},{8,72},{72,8},{16,80},{80,16},{24,88},{88,24},{32,96... | collective-permute-start | bytes 786440 | tf_op jit(solution)/shard_map/ppermute | solution.py:16
  237.2 14.7 %collective-permute-start.4 = (bf16[2,128,1024]{2,1,0:T(8,128)(2,1)S(1)}, bf16[2,128,1024]{2,1,0:T(8,128)(2,1)S(1)}, u32[]{:S(2)}, u32[]{:S(2)}) collective-permute-start(bf16[2,128,1024]{2,1,0:T(8,128)(2,1)S(1)} %maximum_select_fusion.2), channel_id=1, source_target_pairs={{0,128},{128,0},{8,136},{136,8},{16,144},{144,16},{24,152},{152,24... | collective-permute-start | bytes 1572872 | tf_op jit(solution)/shard_map/ppermute | solution.py:16
  252.1 134.6 %collective-permute-start.5 = (bf16[4,128,1024]{2,1,0:T(8,128)(2,1)S(1)}, bf16[4,128,1024]{2,1,0:T(8,128)(2,1)S(1)}, u32[]{:S(2)}, u32[]{:S(2)}) collective-permute-start(bf16[4,128,1024]{2,1,0:T(8,128)(2,1)S(1)} %maximum_select_fusion.1), channel_id=1, source_target_pairs={{0,256},{256,0},{8,264},{264,8},{16,272},{272,16},{24,280},{280,24... | collective-permute-start | bytes 3145736 | tf_op jit(solution)/shard_map/ppermute | solution.py:16
  409.7 0.7 copy-start.3
  409.7 2.6 copy-start.2
Sparse Core Ops, SparseCore 0:
  409.9 40.2 reduce-scatter.3
where the time goes:
time: 461 us; the launch traced here: 460 us
  waiting for transfers between devices  287 us (62%)
  blocking collectives  87.5 us (19%)
  local copies, waits for them, and re-layouts  22.1 us (5%)
  other arithmetic  21.2 us (5%)
  starting transfers between devices  20.9 us (5%)
  between operations  15 us (3%)
  matrix products  6.16 us (1%)
    ppermute x6, waiting for transfers between devices, swapped(): return lax.ppermute(block, axis, route)  249 us
    all_to_all x1, blocking collectives, shards(): lax.all_to_all(own_tile[None], 'pair', split_axis=2, concat_axis=0, tiled...  50.3 us
    unnamed x2, waiting for transfers between devices  37.5 us
    all_to_all x1, blocking collectives, shards(): lax.all_to_all(spread, 'pair', split_axis=0, concat_axis=2, tiled=True)[0]  37.3 us
    unnamed x13, local copies, waits for them, and re-layouts  21.4 us
    ppermute x6, starting transfers between devices, swapped(): return lax.ppermute(block, axis, route)  20.9 us
    select_n x3, other arithmetic, shards(): jnp.where(lower_half, jnp.concatenate([cycle_stack, partner], axis=0), jn...  18.3 us
  transfers between devices with their start and end apart: 7, of which 6 were waited for; matrix products, arithmetic and copies ran while one was open for 3% of the time, Pallas kernels for 0%

commit v1 on v0

--- a/solution.py
+++ b/solution.py
@@ -1,9 +1,23 @@
+import functools
 import math
 
 import jax
 import jax.numpy as jnp
 from jax import lax
+from jax.experimental import pallas as pl
+from jax.experimental.pallas import tpu as pltpu
 from jax.sharding import PartitionSpec as P
+
+MESH = pl.DeviceIdType.MESH
+BF = jnp.bfloat16
+F32 = jnp.float32
+
+NX, NZ, NY = 4, 16, 4
+O = 8
+NV = 8
+V = 1024
+BV = 128
+CAP = 288
 
 
 def swapped(block, axis, stride):
@@ -20,7 +34,7 @@
     return position // 2**level % 2
 
 
-def shards(amplitudes, w_ovvo, occ_irreps, vir_irreps):
+def general(amplitudes, w_ovvo, occ_irreps, vir_irreps):
     own_tile = amplitudes[:, 0]
     devices = lax.axis_size("pair")
     tiles_side = math.isqrt(devices)
@@ -31,9 +45,7 @@
     spread = spread.reshape((tiles_side, tiles_side) + shape_rest)
     spread = jnp.swapaxes(spread, 0, 1).reshape((devices,) + shape_rest)
     mirrored = lax.all_to_all(spread, "pair", split_axis=0, concat_axis=2, tiled=True)[0]
-    cycle_tile = (2.0 * own_tile.astype(jnp.float32) - mirrored.astype(jnp.float32)).astype(
-        jnp.bfloat16
-    )
+    cycle_tile = (2.0 * own_tile.astype(F32) - mirrored.astype(F32)).astype(BF)
     cycle_stack = cycle_tile[None]
     for level in range(bit_count):
         partner = swapped(cycle_stack, "pair", level)
@@ -53,11 +65,11 @@
             jnp.concatenate([partner, weight_stack], axis=0),
         )
     partial_value = jnp.einsum(
-        "kxac,kcb->xab", cycle_stack, weight_stack, preferred_element_type=jnp.float32
+        "kxac,kcb->xab", cycle_stack, weight_stack, preferred_element_type=F32
     )
     summed = lax.psum_scatter(
-        partial_value.astype(jnp.bfloat16), "virt", scatter_dimension=2, tiled=True
-    ).astype(jnp.float32)
+        partial_value.astype(BF), "virt", scatter_dimension=2, tiled=True
+    ).astype(F32)
     width_local = summed.shape[2]
     occ_order = jnp.arange(occ_irreps.shape[0], dtype=jnp.int32)
     left_irrep = jnp.sum(jnp.where(occ_order == position // tiles_side, occ_irreps, 0))
@@ -67,7 +79,413 @@
     )
     target = jnp.bitwise_xor(left_irrep, right_irrep)
     allowed = jnp.bitwise_xor(vir_irreps[:, None], column_irreps[None, :]) == target
-    result = jnp.where(allowed[None], summed, 0.0).astype(jnp.bfloat16)
+    return jnp.where(allowed[None], summed, 0.0).astype(BF)
+
+
+def packed_kernel(
+    starts_ref, colb_ref, amp_ref, w_ref, out_ref,
+    T, S, W, R, cyc, C, Pk, U, D, Fin,
+    t_send, t_recv, t_loc, a_send, a_recv, a_loc, f_send, s_send, s_recv,
+    w2_send, w2_recv, w3_send, w3_recv, w3f_send, w3f_recv, y_send, y_recv,
+    u_send, u_recv, d_send, d_recv,
+):
+    pair, v = lax.axis_index("pair"), lax.axis_index("virt")
+    x, z = pair // NZ, pair % NZ
+    half, l = z // O, z % O
+    y, core = v // 2, v % 2
+
+    def remote(src, dst, send, recv, p, q):
+        return pltpu.make_async_remote_copy(
+            src_ref=src, dst_ref=dst, send_sem=send, recv_sem=recv,
+            device_id=(p, q), device_id_type=MESH,
+        )
+
+    def at(px, pz):
+        return px * NZ + pz
+
+    bar = pltpu.get_barrier_semaphore()
+
+    def greet(p, q):
+        pl.semaphore_signal(bar, inc=1, device_id=(p, q), device_id_type=MESH)
+
+    for d in range(1, NV):
+        greet(pair, (v + d) % NV)
+    for d in range(1, NX):
+        greet(at((x + d) % NX, z), v)
+    for j in range(O):
+        source = O * (l % 2) + j
+
+        @pl.when(source != z)
+        def _():
+            greet(at(x, source), v)
+
+    @pl.when(l > 0)
+    def _():
+        greet(at(x, z - 1), v)
+
+    @pl.when(l < O - 1)
+    def _():
+        greet(at(x, z + 1), v)
+
+    own_k = (l % 2 == half).astype(jnp.int32)
+    ends = (l > 0).astype(jnp.int32) + (l < O - 1).astype(jnp.int32)
+    pl.semaphore_wait(bar, (NV - 1) + (NX - 1) + O - own_k + ends)
+
+    my_rows = pl.ds(pl.multiple_of(v * BV, BV), BV)
+
+    def w_piece(q):
+        return w_ref.at[0, :, pl.ds(pl.multiple_of(q * BV, BV), BV)]
+
+    def t_copy(d):
+        q = (v + d) % NV
+        return remote(w_piece(q), T.at[my_rows], t_send.at[d - 1], t_recv.at[d - 1], pair, q)
+
+    for d in range(1, NV):
+        t_copy(d).start()
+    t_local = pltpu.make_async_copy(w_piece(v), T.at[my_rows], t_loc)
+    t_local.start()
+    t_local.wait()
+    for d in range(1, NV):
+        t_copy(d).wait_recv()
+
+    XR = V // NX
+
+    def quarter(q):
+        return pl.ds(pl.multiple_of(q * XR, XR), XR)
+
+    def s_copy(d):
+        q = (x + d) % NX
+        return remote(T.at[quarter(q)], S.at[x], s_send.at[d - 1], s_recv.at[d - 1], at(q, z), v)
+
+    for d in range(1, NX):
+        s_copy(d).start()
+
+    a_local = pltpu.make_async_copy(amp_ref.at[core, 0], R.at[v], a_loc)
+    a_local.start()
+
+    def a_sibling():
+        return remote(amp_ref.at[1 - core, 0], R.at[v], a_send.at[4], a_recv.at[v], pair, v + 1 - 2 * core)
+
+    def a_copy(dy, cc):
+        return remote(
+            amp_ref.at[cc, 0], R.at[v], a_send.at[(dy // 2) * 2 + cc], a_recv.at[v],
+            pair, ((y + dy) % NY) * 2 + cc,
+        )
+
+    def a_arrived(g):
+        remote(R.at[g], R.at[g], a_send.at[0], a_recv.at[g], pair, v + 1 - 2 * core).wait_recv()
+
+    a_sibling().start()
+    for cc in range(2):
+        for dy in (1, 3):
+            a_copy(dy, cc).start()
+
+    def w2_copy(d, h):
+        q = (x - d + NX) % NX
+        src = T.at[quarter(x)] if d == 0 else S.at[q]
+        dz = 2 * q + half + O * h
+        return src, dz, remote(
+            src, W.at[l, quarter(x)], w2_send.at[2 * d + h], w2_recv.at[l], at(x, dz), v
+        )
+
+    for d in range(NX):
+        if d:
+            s_copy(d).wait_recv()
+        for h in range(2):
+            src, dz, copy = w2_copy(d, h)
+
+            @pl.when(dz != z)
+            def _():
+                copy.start()
+
+            @pl.when(dz == z)
+            def _():
+                pltpu.make_async_copy(src, W.at[l, quarter(x)], w2_recv.at[l]).start()
+
+    g_lo = ((y + 3) % NY) * 2
+    g_hi = ((y + 1) % NY) * 2 + 1
+
+    def f_copy(i):
+        g, dy = ((g_lo, 1), (g_hi, 3))[i]
+        return remote(R.at[g], R.at[g], f_send.at[i], a_recv.at[g], pair, ((y + dy) % NY) * 2 + core)
+
+    a_arrived(g_lo)
+    f_copy(0).start()
+    a_arrived(g_hi)
+    f_copy(1).start()
+
+    def cycle_part(part, blocks):
+        def body(i, carry):
+            r = part * blocks + i
+            row = pl.ds(pl.multiple_of(r * BV, BV), BV)
+            for q in range(NV):
+                mine = R[q, row, :].astype(F32)
+                other = R[r, q * BV:(q + 1) * BV, :].astype(F32)
+                cyc[core, row, q * BV:(q + 1) * BV] = (2.0 * mine - other.T).astype(BF)
+            return carry
+
+        lax.fori_loop(0, blocks, body, 0)
+
+    def y_copy(part):
+        rows = pl.ds(part * 256, 256)
+        return remote(
+            cyc.at[core, rows], cyc.at[core, rows], y_send.at[part], y_recv.at[part], pair, v + 1 - 2 * core
+        )
+
+    near = half == l % 2
+
+    def order(n):
+        offset = (0, 1, -1, 2, -2, 3, -3, 4)
+        step = jnp.where(near, offset[n], offset[O - 1 - n])
+        return (l + step + O) % O
+
+    def w3_copy(n, way):
+        j = order(n)
+        block = W.at[j, quarter(x)]
+        q = (x + (1, 3)[way]) % NX
+        return remote(block, block, w3_send.at[way, n], w3_recv.at[way, j], at(q, z), v)
+
+    def w3_arrived(n, way):
+        j = order(n)
+        block = W.at[j, quarter((x + (3, 1)[way]) % NX)]
+        remote(block, block, w3_send.at[way, n], w3_recv.at[way, j], pair, v + 1 - 2 * core).wait_recv()
+
+    def w3_forward(n):
+        way = n % 2
+        j = order(n)
+        block = W.at[j, quarter((x + (3, 1)[way]) % NX)]
+        q = (x + (1, 3)[way]) % NX
+        return remote(block, block, w3f_send.at[n], w3f_recv.at[j], at(q, z), v)
+
+    for n in range(O + 1):
+        if n < O:
+            j = order(n)
+            block = W.at[j, quarter(x)]
+            pltpu.make_async_copy(block, block, w2_recv.at[j]).wait()
+            for way in range(2):
+                w3_copy(n, way).start()
+        if n > 0:
+            w3_arrived(n - 1, (n - 1) % 2)
+            w3_forward(n - 1).start()
+        if n == 3:
+            a_local.wait()
+            a_arrived(v + 1 - 2 * core)
+            a_arrived(g_lo + 1)
+            a_arrived(g_hi - 1)
+            a_arrived(((y + 2) % NY) * 2)
+            a_arrived(((y + 2) % NY) * 2 + 1)
+        if 3 <= n < 7:
+            cycle_part(n - 3, 2)
+            y_copy(n - 3).start()
+    for n in range(O):
+        w3_arrived(n, 1 - n % 2)
+    for n in range(O):
+        j = order(n)
+        block = W.at[j, quarter((x + 2) % NX)]
+        pltpu.make_async_copy(block, block, w3f_recv.at[j]).wait()
+    for part in range(4):
+        rows = pl.ds(part * 256, 256)
+        block = cyc.at[1 - core, rows]
+        pltpu.make_async_copy(block, block, y_recv.at[part]).wait()
+
+    colb = jnp.broadcast_to(colb_ref[0:1, :], (CAP, BV))
+
+    def products(s):
+        weights = jnp.concatenate([W[O - 1 - s], W[s]], axis=1)
+
+        def body(i, carry):
+            xx, m = i // 4, i % 4
+            rows = pl.ds(pl.multiple_of(m * 256, 256), 256)
+            value = jnp.dot(cyc[xx, rows, :], weights, preferred_element_type=F32)
+            C[pl.ds(pl.multiple_of(i * 256, 256), 256), :] = value[:, :BV]
+            C[pl.ds(pl.multiple_of(i * 256 + 2 * V, 256), 256), :] = value[:, BV:]
+            return carry
+
+        lax.fori_loop(0, 8, body, 0)
+
+        for side in range(2):
+            j = (O - 1 - s, s)[side]
+            for xx in range(2):
+                acc = jnp.zeros((CAP, BV), F32)
+                for beta in range(O):
+                    start = starts_ref[j, beta] * 8 + (side * 2 + xx) * V
+                    acc = jnp.where(colb == beta, C[pl.ds(start, CAP), :], acc)
+                Pk[j, xx] = acc.astype(BF)
+
+    def hop(buf, send, recv, j, xx, step):
+        return remote(buf.at[j, xx], buf.at[j, xx], send.at[j, xx], recv.at[j, xx], at(x, z + step), v)
+
+    def flow(buf, send, recv, j, xx, step, first):
+        @pl.when(first)
+        def _():
+            buf[j, xx] = Pk[j, xx]
+
+        @pl.when(jnp.logical_not(first))
+        def _():
+            hop(buf, send, recv, j, xx, step).wait_recv()
+            buf[j, xx] = (buf[j, xx].astype(F32) + Pk[j, xx].astype(F32)).astype(BF)
+
+        hop(buf, send, recv, j, xx, step).start()
+
+    def tick(tau, carry):
+        @pl.when(tau < 4)
+        def _():
+            products(tau)
+
+        for xx in range(2):
+            @pl.when(tau >= l)
+            def _():
+                flow(U, u_send, u_recv, O - 1 + l - tau, xx, 1, l == 0)
+
+            @pl.when(tau >= O - 1 - l)
+            def _():
+                flow(D, d_send, d_recv, l - (O - 1 - tau), xx, -1, l == O - 1)
+
+        return carry
+
+    lax.fori_loop(0, O - 1, tick, 0)
+
+    Fin[...] = Pk[l].astype(F32)
+    for xx in range(2):
+        @pl.when(l > 0)
+        def _():
+            hop(U, u_send, u_recv, l, xx, 1).wait_recv()
+            Fin[xx] += U[l, xx].astype(F32)
+
+        @pl.when(l < O - 1)
+        def _():
+            hop(D, d_send, d_recv, l, xx, -1).wait_recv()
+            Fin[xx] += D[l, xx].astype(F32)
+
+    out_ref[...] = Fin[...].astype(BF)
+
+    for d in range(1, NV):
+        t_copy(d).wait_send()
+    for d in range(1, NX):
+        s_copy(d).wait_send()
+    a_sibling().wait_send()
+    for cc in range(2):
+        for dy in (1, 3):
+            a_copy(dy, cc).wait_send()
+    for d in range(NX):
+        for h in range(2):
+            _, dz, copy = w2_copy(d, h)
+
+            @pl.when(dz != z)
+            def _():
+                copy.wait_send()
+    for i in range(2):
+        f_copy(i).wait_send()
+    for n in range(O):
+        w3_copy(n, 0).wait_send()
+        w3_copy(n, 1).wait_send()
+        w3_forward(n).wait_send()
+    for part in range(4):
+        y_copy(part).wait_send()
+
+    def drain(j, carry):
+        for xx in range(2):
+            @pl.when(j > l)
+            def _():
+                hop(U, u_send, u_recv, j, xx, 1).wait_send()
+
+            @pl.when(j < l)
+            def _():
+                hop(D, d_send, d_recv, j, xx, -1).wait_send()
+
+        return carry
+
+    lax.fori_loop(0, O, drain, 0)
+
+
+def unpack_kernel(start_ref, begin_ref, end_ref, target_ref, colb_ref, packed_ref, out_ref, wide):
+    target = target_ref[0]
+    STEP = 32
+    wide[:, STEP:STEP + CAP, :] = packed_ref[...].astype(F32)
+    colb = jnp.broadcast_to(colb_ref[0:1, :], (STEP, BV))
+    row = lax.broadcasted_iota(jnp.int32, (STEP, BV), 0)
+
+    def body(i, carry):
+        first = pl.multiple_of(i * STEP, STEP)
+        acc = [jnp.zeros((STEP, BV), F32)] * 2
+        for alpha in range(O):
+            at = jnp.clip(first - start_ref[alpha], -STEP, CAP) + STEP
+            at = pl.multiple_of(at, 8)
+            inside = (row + first >= begin_ref[alpha]) & (row + first < end_ref[alpha])
+            inside = inside & (colb == jnp.bitwise_xor(target, alpha))
+            for xx in range(2):
+                acc[xx] = jnp.where(inside, wide[xx, pl.ds(at, STEP), :], acc[xx])
+        for xx in range(2):
+            out_ref[xx, pl.ds(first, STEP), :] = acc[xx].astype(BF)
+        return carry
+
+    lax.fori_loop(0, V // STEP, body, 0)
+
+
+def packed(tables, amplitudes, w_ovvo):
+    starts, start, begin, end, target, colb = tables
+    smem = pl.BlockSpec(memory_space=pltpu.SMEM)
+    vmem = pl.BlockSpec(memory_space=pltpu.VMEM)
+    anym = pl.BlockSpec(memory_space=pl.ANY)
+    dma = pltpu.SemaphoreType.DMA
+    small = pl.pallas_call(
+        packed_kernel,
+        out_shape=jax.ShapeDtypeStruct((2, CAP, BV), BF),
+        in_specs=[smem, vmem, anym, anym],
+        out_specs=vmem,
+        scratch_shapes=[
+            pltpu.VMEM((V, BV), BF),
+            pltpu.VMEM((NX, V // NX, BV), BF),
+            pltpu.VMEM((O, V, BV), BF),
+            pltpu.VMEM((NV, V, BV), BF),
+            pltpu.VMEM((2, V, V), BF),
+            pltpu.VMEM((4 * V, BV), F32),
+            pltpu.VMEM((O, 2, CAP, BV), BF),
+            pltpu.VMEM((O, 2, CAP, BV), BF),
+            pltpu.VMEM((O, 2, CAP, BV), BF),
+            pltpu.VMEM((2, CAP, BV), F32),
+            dma((7,)), dma((7,)), dma, dma((5,)), dma((NV,)), dma, dma((2,)), dma((3,)), dma((3,)),
+            dma((8,)), dma((O,)), dma((2, O)), dma((2, O)), dma((O,)), dma((O,)), dma((4,)), dma((4,)),
+            dma((O, 2)), dma((O, 2)), dma((O, 2)), dma((O, 2)),
+        ],
+        compiler_params=pltpu.CompilerParams(
+            collective_id=0, has_side_effects=True, vmem_limit_bytes=40 * 2**20
+        ),
+        name="packed_cycle",
+    )(starts, colb, amplitudes, w_ovvo)
+    return pl.pallas_call(
+        unpack_kernel,
+        out_shape=jax.ShapeDtypeStruct((2, V, BV), BF),
+        in_specs=[smem, smem, smem, smem, vmem, vmem],
+        out_specs=vmem,
+        scratch_shapes=[pltpu.VMEM((2, CAP + 64, BV), F32)],
+        name="unpack",
+    )(start, begin, end, target, colb, small)
+
+
+def shards(amplitudes, w_ovvo, occ_irreps, vir_irreps):
+    position = lax.axis_index("pair")
+    left, right = position // O, position % O
+    irreps = jnp.arange(O, dtype=jnp.int32)
+    below = vir_irreps[None, :] < irreps[:, None]
+    upto = vir_irreps[None, :] <= irreps[:, None]
+    begin = jnp.sum(below.astype(jnp.int32), axis=1)
+    end = jnp.sum(upto.astype(jnp.int32), axis=1)
+    start = jnp.minimum(begin // 8 * 8, V - CAP)
+    fits = jnp.all(end - start <= CAP)
+    occ_left = jnp.sum(jnp.where(irreps == left, occ_irreps, 0))
+    occ_right = jnp.sum(jnp.where(irreps == right, occ_irreps, 0))
+    target = jnp.bitwise_xor(occ_left, occ_right)[None]
+    alpha = jnp.bitwise_xor(jnp.bitwise_xor(occ_left, occ_irreps)[:, None], irreps[None, :])
+    starts = jnp.sum(jnp.where(alpha[:, :, None] == irreps, start // 8, 0), axis=2)
+    colb = lax.dynamic_slice_in_dim(vir_irreps, lax.axis_index("virt") * BV, BV)
+    colb = jnp.broadcast_to(colb[None, :], (8, BV))
+    tables = (starts, start, begin, end, target, colb)
+    result = lax.cond(
+        fits,
+        lambda: packed(tables, amplitudes, w_ovvo),
+        lambda: general(amplitudes, w_ovvo, occ_irreps, vir_irreps),
+    )
     return result[:, None]
 
 

time: 461 us -> 129 us (0.28)
  the two profiles are of different devices: /device:TPU:6 before, /device:TPU:34 now
where the time goes in v1:
time: 129 us; the launch traced here: 128 us
  Pallas kernels  106 us (82%)
  between operations  14.1 us (11%)
  other arithmetic  4.46 us (3%)
  local copies, waits for them, and re-layouts  2.24 us (2%)
  loops' own time  1.49 us (1%)
    pallas_call x1, Pallas kernels, packed(): pl.pallas_call(packed_kernel, out_shape=jax.ShapeDtypeStruct((2, CAP, BV)...  104 us

profile of v1, /device:TPU:34, one launch (start us, length us, event | category | flops | bytes accessed | tf_op | source)
XLA Modules:
  0.0 128.3 jit_solution(15257595407702960197)
XLA Ops:
  6.5 0.8 convert_reduce_fusion
  7.4 0.7 compare_reduce_fusion
  8.7 111.9 %conditional.1 = (bf16[2,1,1024,128]{3,2,0,1:T(8,128)(2,1)S(1)}) conditional(s32[]{:T(128)} %convert_element_type.59, (s32[1024]{0:T(1024)}, s32[8]{0:T(128)}, bf16[2,1,1024,128]{3,2,1,0:T(8,128)(2,1)}, bf16[1,128,1024]{2,1,0:T(8,128)(2,1)}) %tuple.43, (s32[]{:T(128)}, s32[]{:T(128)}, s32[]{:T(128)}, s32[8]{0:T(128)S(1)}, s32[8]{0:T(128)}, ...), branch_computations={%region_3.7_spmd, %region_7.11_spmd} | conditional | flops 4315938816 | bytes 97803624 | solution.py:484
  9.0 1.3 %fusion.17 = (s32[]{:T(128)}, s32[]{:T(128)}, s32[8]{0:T(128)S(1)}) fusion(s32[8]{0:T(128)} %get-tuple-element.168, s32[8]{0:T(128)S(1)} %get-tuple-element.227, s32[8]{0:T(128)S(1)} %get-tuple-element.170, s32[]{:T(128)S(6)} %select_n.140, s32[8]{0:T(128)S(1)} %get-tuple-element.170, s32[]{:T(128)S(6)} %select_n.138, s32[8]{0:T(128)S(1)} %get-tuple-element.179, ...), kind=kLoop, calls=%fused_computation.36 | loop fusion | flops 166 | bytes 368 | tf_op jit(solution)/shard_map/reduce_sum | solution.py:477
  10.3 1.3 %broadcast_xor_fusion = s32[8]{0:T(128)S(1)} fusion(s32[8]{0:T(128)} %get-tuple-element.168, s32[]{:T(128)} %get-tuple-element.206), kind=kLoop, calls=%fused_computation.37 | loop fusion | flops 8 | bytes 68 | tf_op jit(solution)/shard_map/xor | solution.py:479
  11.6 0.1 xor_bitcast_fusion
  11.7 0.3 select_reduce_fusion.starts_ref
  12.0 0.8 dynamic_slice.6
  12.8 0.0 copy-start.1
  12.8 103.5 %packed_cycle.1.packed_ref = bf16[2,288,128]{2,1,0:T(8,128)(2,1)S(1)} custom-call(s32[8,8]{1,0:T(8,128)S(1)} %select_reduce_fusion.starts_ref, s32[8,128]{1,0:T(8,128)S(1)} %broadcast_in_dim.55.colb_ref, bf16[2,1,1024,128]{3,2,1,0:T(8,128)(2,1)} %get-tuple-element.180.amp_ref, bf16[1,128,1024]{2,1,0:T(8,128)(2,1)} %get-tuple-element.181.w_ref), custom_call_target="tpu_custom_call" | custom-call | tf_op jit(solution)/shard_map/cond/branch_1_fun/packed_cycle/pallas_call | solution.py:431
  116.3 0.0 copy-start
  116.3 0.7 copy-done
  118.1 0.0 copy-done.1
  118.2 2.5 %unpack.1 = bf16[2,1024,128]{2,1,0:T(8,128)(2,1)S(1)} custom-call(s32[8]{0:T(128)S(1)} %get-tuple-element.186, s32[8]{0:T(128)S(1)} %get-tuple-element.162.begin_ref, s32[8]{0:T(128)S(1)} %get-tuple-element.163.end_ref, s32[1]{0:T(128)} %bitcast.13.target_ref, s32[8,128]{1,0:T(8,128)} %copy-done.1, bf16[2,288,128]{2,1,0:T(8,128)(2,1)} %copy-done), custom_call_target="tpu_custom_call" | custom-call | tf_op jit(solution)/shard_map/cond/branch_1_fun/unpack/pallas_call | solution.py:456
  120.7 0.0 copy-start.4
  120.7 0.8 copy-done.4
  (9 shorter events, 0.0 us)
Async XLA Ops:
  12.8 105.4 %copy-start.1 = (s32[8,128]{1,0:T(8,128)}, s32[8,128]{1,0:T(8,128)S(1)}, u32[]{:S(2)}) copy-start(s32[8,128]{1,0:T(8,128)S(1)} %broadcast_in_dim.55.colb_ref) | copy-start | bytes 12292 | tf_op jit(solution)/shard_map/cond
  116.3 0.7 copy-start
  120.7 0.8 copy-start.4

commit v2 on v0

--- a/solution.py
+++ b/solution.py
@@ -1,9 +1,23 @@
+import functools
 import math
 
 import jax
 import jax.numpy as jnp
 from jax import lax
+from jax.experimental import pallas as pl
+from jax.experimental.pallas import tpu as pltpu
 from jax.sharding import PartitionSpec as P
+
+MESH = pl.DeviceIdType.MESH
+BF = jnp.bfloat16
+F32 = jnp.float32
+
+NX, NZ, NY = 4, 16, 4
+O = 8
+NV = 8
+V = 1024
+BV = 128
+CAP = 288
 
 
 def swapped(block, axis, stride):
@@ -20,7 +34,7 @@
     return position // 2**level % 2
 
 
-def shards(amplitudes, w_ovvo, occ_irreps, vir_irreps):
+def general(amplitudes, w_ovvo, occ_irreps, vir_irreps):
     own_tile = amplitudes[:, 0]
     devices = lax.axis_size("pair")
     tiles_side = math.isqrt(devices)
@@ -31,9 +45,7 @@
     spread = spread.reshape((tiles_side, tiles_side) + shape_rest)
     spread = jnp.swapaxes(spread, 0, 1).reshape((devices,) + shape_rest)
     mirrored = lax.all_to_all(spread, "pair", split_axis=0, concat_axis=2, tiled=True)[0]
-    cycle_tile = (2.0 * own_tile.astype(jnp.float32) - mirrored.astype(jnp.float32)).astype(
-        jnp.bfloat16
-    )
+    cycle_tile = (2.0 * own_tile.astype(F32) - mirrored.astype(F32)).astype(BF)
     cycle_stack = cycle_tile[None]
     for level in range(bit_count):
         partner = swapped(cycle_stack, "pair", level)
@@ -53,11 +65,12 @@
             jnp.concatenate([partner, weight_stack], axis=0),
         )
     partial_value = jnp.einsum(
-        "kxac,kcb->xab", cycle_stack, weight_stack, preferred_element_type=jnp.float32
+        "kxac,kcb->xab", cycle_stack, weight_stack, preferred_element_type=F32
     )
-    summed = lax.psum_scatter(
-        partial_value.astype(jnp.bfloat16), "virt", scatter_dimension=2, tiled=True
-    ).astype(jnp.float32)
+    pieces = lax.all_to_all(
+        partial_value.astype(BF)[None], "virt", split_axis=3, concat_axis=0, tiled=True
+    )
+    summed = jnp.sum(pieces.astype(F32), axis=0)
     width_local = summed.shape[2]
     occ_order = jnp.arange(occ_irreps.shape[0], dtype=jnp.int32)
     left_irrep = jnp.sum(jnp.where(occ_order == position // tiles_side, occ_irreps, 0))
@@ -67,7 +80,448 @@
     )
     target = jnp.bitwise_xor(left_irrep, right_irrep)
     allowed = jnp.bitwise_xor(vir_irreps[:, None], column_irreps[None, :]) == target
-    result = jnp.where(allowed[None], summed, 0.0).astype(jnp.bfloat16)
+    return jnp.where(allowed[None], summed, 0.0).astype(BF)
+
+
+PAD = 32
+FR = CAP + 2 * PAD
+NG = 4
+GW = V // NG
+
+
+def packed_kernel(
+    occ_ref, vir_ref, amp_ref, w_ref, out_ref, fits_ref,
+    T, S, W, R, cyc, C, Pk, U, D, Fin, key, st,
+    t_send, t_recv, a_send, a_recv, f_send, s_send, s_recv,
+    w2_send, w2_recv, w3_send, w3_recv, w3f_send, w3f_recv, y_send, y_recv,
+    u_send, u_recv, d_send, d_recv,
+):
+    pair, v = lax.axis_index("pair"), lax.axis_index("virt")
+    x, z = pair // NZ, pair % NZ
+    half, l = z // O, z % O
+    y, core = v // 2, v % 2
+    sibling = v + 1 - 2 * core
+
+    def remote(src, dst, send, recv, p, q):
+        return pltpu.make_async_remote_copy(
+            src_ref=src, dst_ref=dst, send_sem=send, recv_sem=recv,
+            device_id=(p, q), device_id_type=MESH,
+        )
+
+    def arrived(block, sem):
+        pltpu.make_async_copy(block, block, sem).wait()
+
+    def at(px, pz):
+        return px * NZ + pz
+
+    bar = pltpu.get_barrier_semaphore()
+
+    def greet(p, q):
+        pl.semaphore_signal(bar, inc=1, device_id=(p, q), device_id_type=MESH)
+
+    for d in range(1, NV):
+        greet(pair, (v + d) % NV)
+    for d in range(1, NX):
+        greet(at((x + d) % NX, z), v)
+    for j in range(O):
+        source = O * (l % 2) + j
+
+        @pl.when(source != z)
+        def _():
+            greet(at(x, source), v)
+
+    @pl.when(l > 0)
+    def _():
+        greet(at(x, z - 1), v)
+
+    @pl.when(l < O - 1)
+    def _():
+        greet(at(x, z + 1), v)
+
+    own_k = (l % 2 == half).astype(jnp.int32)
+    ends = (l > 0).astype(jnp.int32) + (l < O - 1).astype(jnp.int32)
+    pl.semaphore_wait(bar, (NV - 1) + (NX - 1) + O - own_k + ends)
+
+    def w_piece(q):
+        return w_ref.at[0, :, pl.ds(pl.multiple_of(q * BV, BV), BV)]
+
+    def t_copy(d):
+        q = (v + d) % NV
+        return remote(w_piece(q), T.at[v], t_send.at[d - 1], t_recv.at[v], pair, q)
+
+    t_local = pltpu.make_async_copy(w_piece(v), T.at[v], t_recv.at[v])
+    t_local.start()
+    for d in range(1, NV):
+        t_copy(d).start()
+
+    a_local = pltpu.make_async_copy(amp_ref.at[core, 0], R.at[v], a_recv.at[v])
+    a_local.start()
+
+    def a_sibling():
+        return remote(amp_ref.at[1 - core, 0], R.at[v], a_send.at[4], a_recv.at[v], pair, sibling)
+
+    def a_copy(dy, cc):
+        return remote(
+            amp_ref.at[cc, 0], R.at[v], a_send.at[(dy // 2) * 2 + cc], a_recv.at[v],
+            pair, ((y + dy) % NY) * 2 + cc,
+        )
+
+    def a_arrived(g):
+        arrived(R.at[g], a_recv.at[g])
+
+    a_sibling().start()
+    for cc in range(2):
+        for dy in (1, 3):
+            a_copy(dy, cc).start()
+
+    XR = BV // NX
+
+    def chunk(n):
+        return (y + n) % NY
+
+    def blocks(n):
+        return pl.ds(2 * chunk(n), 2)
+
+    def quarter(q):
+        return pl.ds(pl.multiple_of(q * XR, XR), XR)
+
+    def s_copy(n, d):
+        q = (x + d) % NX
+        return remote(
+            T.at[blocks(n), quarter(q)], S.at[x, blocks(n)],
+            s_send.at[n, d - 1], s_recv.at[n, d - 1], at(q, z), v,
+        )
+
+    def spread_x(n):
+        for i in range(2):
+            g = 2 * chunk(n) + i
+            arrived(T.at[g], t_recv.at[g])
+        for d in range(1, NX):
+            s_copy(n, d).start()
+
+    def w2_copy(n, d, h):
+        q = (x - d + NX) % NX
+        src = T.at[blocks(n), quarter(x)] if d == 0 else S.at[q, blocks(n)]
+        dst = W.at[l, blocks(n), quarter(x)]
+        dz = 2 * q + half + O * h
+        return dz, src, dst, remote(src, dst, w2_send.at[n, 2 * d + h], w2_recv.at[n, l], at(x, dz), v)
+
+    def move_z(n):
+        for d in range(NX):
+            if d:
+                q = (x - d + NX) % NX
+                arrived(S.at[q, blocks(n)], s_recv.at[n, d - 1])
+            for h in range(2):
+                dz, src, dst, copy = w2_copy(n, d, h)
+
+                @pl.when(dz != z)
+                def _():
+                    copy.start()
+
+                @pl.when(dz == z)
+                def _():
+                    pltpu.make_async_copy(src, dst, w2_recv.at[n, l]).start()
+
+    def left_z(n):
+        for d in range(NX):
+            for h in range(2):
+                dz, _, _, copy = w2_copy(n, d, h)
+
+                @pl.when(dz != z)
+                def _():
+                    copy.wait_send()
+
+    def w3_copy(n, way):
+        block = W.at[:, blocks(n), quarter(x)]
+        return remote(block, block, w3_send.at[n, way], w3_recv.at[n, way], at((x + (1, 3)[way]) % NX, z), v)
+
+    def gather_x(n):
+        for j in range(O):
+            arrived(W.at[j, blocks(n), quarter(x)], w2_recv.at[n, j])
+        for way in range(2):
+            w3_copy(n, way).start()
+
+    def w3_forward(n, way):
+        block = W.at[pl.ds(4 * way, 4), blocks(n), quarter((x + (3, 1)[way]) % NX)]
+        return remote(block, block, w3f_send.at[n, way], w3f_recv.at[n, way], at((x + (1, 3)[way]) % NX, z), v)
+
+    def forward_x(n):
+        for way in range(2):
+            arrived(W.at[:, blocks(n), quarter((x + (3, 1)[way]) % NX)], w3_recv.at[n, way])
+            w3_forward(n, way).start()
+
+    def gathered_x(n):
+        for way in range(2):
+            arrived(W.at[pl.ds(4 * way, 4), blocks(n), quarter((x + 2) % NX)], w3f_recv.at[n, way])
+
+    g_lo = ((y + 3) % NY) * 2
+    g_hi = ((y + 1) % NY) * 2 + 1
+
+    def f_copy(i):
+        g, dy = ((g_lo, 1), (g_hi, 3))[i]
+        return remote(R.at[g], R.at[g], f_send.at[i], a_recv.at[g], pair, ((y + dy) % NY) * 2 + core)
+
+    def cycle_part(part):
+        def body(i, carry):
+            r = part * 2 + i
+            row = pl.ds(pl.multiple_of(r * BV, BV), BV)
+            for q in range(NV):
+                mine = R[q, row, :].astype(F32)
+                other = R[r, q * BV:(q + 1) * BV, :].astype(F32)
+                cyc[core, row, q * BV:(q + 1) * BV] = (2.0 * mine - other.T).astype(BF)
+            return carry
+
+        lax.fori_loop(0, 2, body, 0)
+        y_copy(part).start()
+
+    def y_copy(part):
+        rows = pl.ds(part * 256, 256)
+        return remote(
+            cyc.at[core, rows], cyc.at[core, rows], y_send.at[part], y_recv.at[part], pair, sibling
+        )
+
+    irreps = vir_ref[...]
+    begin = [jnp.sum((irreps < alpha).astype(jnp.int32)) for alpha in range(1, O)]
+    begin = [jnp.int32(0)] + begin + [jnp.int32(V)]
+
+    def tables():
+        good = jnp.int32(1)
+        for alpha in range(O):
+            first = jnp.minimum(lax.shift_right_logical(begin[alpha], 3), (V - CAP) // 8)
+            st[alpha] = first
+            good = jnp.where(begin[alpha + 1] - first * 8 <= CAP, good, 0)
+        fits_ref[0] = good
+        target = jnp.bitwise_xor(occ_ref[pair // O], occ_ref[pair % O])
+        columns = jnp.bitwise_xor(jnp.broadcast_to(vir_ref[pl.ds(v, 1), :], (BV, BV)), target)
+        row = lax.broadcasted_iota(jnp.int32, (BV, BV), 0)
+
+        def body(i, carry):
+            own = jnp.zeros((BV, BV), jnp.int32)
+            for alpha in range(1, O):
+                own = own + (row + i * BV >= begin[alpha]).astype(jnp.int32)
+            key[pl.ds(pl.multiple_of(i * BV, BV), BV), :] = jnp.where(own == columns, own, -1)
+            return carry
+
+        lax.fori_loop(0, V // BV, body, 0)
+
+    def product(n, s):
+        g = chunk(n)
+        weights = jnp.concatenate(
+            [W[O - 1 - s, blocks(n)].reshape(GW, BV), W[s, blocks(n)].reshape(GW, BV)], axis=1
+        )
+        columns = pl.ds(pl.multiple_of(g * GW, GW), GW)
+
+        def body(xx, carry):
+            for m in range(4):
+                value = jnp.dot(
+                    cyc[xx, pl.ds(m * 256, 256), columns], weights, preferred_element_type=F32
+                )
+                for side in range(2):
+                    j = (O - 1 - s, s)[side]
+                    rows = pl.ds(pl.multiple_of((j * 2 + xx) * V + m * 256, 256), 256)
+                    part = value[:, side * BV:(side + 1) * BV]
+                    C[rows, :] = part if n == 0 else C[rows, :] + part
+            return carry
+
+        lax.fori_loop(0, 2, body, 0)
+
+    def products(n):
+        def body(s, carry):
+            product(n, s)
+            return carry
+
+        lax.fori_loop(0, 4, body, 0)
+
+    for n in range(NG):
+        spread_x(n)
+    move_z(0)
+    move_z(1)
+    tables()
+    a_arrived(g_lo)
+    f_copy(0).start()
+    a_arrived(g_hi)
+    f_copy(1).start()
+    left_z(0)
+    move_z(2)
+    gather_x(0)
+    forward_x(0)
+    left_z(1)
+    move_z(3)
+    gather_x(1)
+    a_arrived(v)
+    a_arrived(sibling)
+    a_arrived(g_lo + 1)
+    a_arrived(g_hi - 1)
+    a_arrived(((y + 2) % NY) * 2)
+    a_arrived(((y + 2) % NY) * 2 + 1)
+    cycle_part(0)
+    cycle_part(1)
+    forward_x(1)
+    gather_x(2)
+    cycle_part(2)
+    cycle_part(3)
+    forward_x(2)
+    gathered_x(0)
+    for part in range(4):
+        arrived(cyc.at[1 - core, pl.ds(part * 256, 256)], y_recv.at[part])
+    products(0)
+    gather_x(3)
+    gathered_x(1)
+    products(1)
+    forward_x(3)
+    gathered_x(2)
+    products(2)
+    gathered_x(3)
+
+    colb = jnp.broadcast_to(vir_ref[pl.ds(v, 1), :], (CAP, BV))
+    occ_left = occ_ref[pair // O]
+
+    def pack(s):
+        for side in range(2):
+            j = (O - 1 - s, s)[side]
+            target = jnp.bitwise_xor(occ_left, occ_ref[j])
+            for xx in range(2):
+                acc = jnp.zeros((CAP, BV), F32)
+                for beta in range(O):
+                    start = st[jnp.bitwise_xor(target, beta)] * 8 + (j * 2 + xx) * V
+                    acc = jnp.where(colb == beta, C[pl.ds(start, CAP), :], acc)
+                Pk[j, xx] = acc.astype(BF)
+
+    def hop(buf, send, recv, j, xx, step):
+        return remote(buf.at[j, xx], buf.at[j, xx], send.at[j, xx], recv.at[j, xx], at(x, z + step), v)
+
+    def flow(buf, send, recv, j, xx, step, first):
+        @pl.when(first)
+        def _():
+            buf[j, xx] = Pk[j, xx]
+
+        @pl.when(jnp.logical_not(first))
+        def _():
+            hop(buf, send, recv, j, xx, step).wait_recv()
+            buf[j, xx] = (buf[j, xx].astype(F32) + Pk[j, xx].astype(F32)).astype(BF)
+
+        hop(buf, send, recv, j, xx, step).start()
+
+    def tick(tau, carry):
+        @pl.when(tau < 4)
+        def _():
+            product(NG - 1, tau)
+            pack(tau)
+
+        for xx in range(2):
+            @pl.when(tau >= l)
+            def _():
+                flow(U, u_send, u_recv, O - 1 + l - tau, xx, 1, l == 0)
+
+            @pl.when(tau >= O - 1 - l)
+            def _():
+                flow(D, d_send, d_recv, l - (O - 1 - tau), xx, -1, l == O - 1)
+
+        return carry
+
+    lax.fori_loop(0, O - 1, tick, 0)
+
+    for xx in range(2):
+        mid = pl.ds(xx * FR + PAD, CAP)
+        Fin[mid, :] = Pk[l, xx].astype(F32)
+
+        @pl.when(l > 0)
+        def _():
+            hop(U, u_send, u_recv, l, xx, 1).wait_recv()
+            Fin[mid, :] += U[l, xx].astype(F32)
+
+        @pl.when(l < O - 1)
+        def _():
+            hop(D, d_send, d_recv, l, xx, -1).wait_recv()
+            Fin[mid, :] += D[l, xx].astype(F32)
+
+        def unpack(i, carry):
+            rows = pl.ds(pl.multiple_of(i * PAD, PAD), PAD)
+            held = key[rows, :]
+            acc = jnp.zeros((PAD, BV), F32)
+            for alpha in range(O):
+                first = jnp.clip(i * (PAD // 8) - st[alpha], -PAD // 8, CAP // 8) + PAD // 8
+                acc = jnp.where(held == alpha, Fin[pl.ds(first * 8 + xx * FR, PAD), :], acc)
+            out_ref[xx, rows, :] = acc.astype(BF)
+            return carry
+
+        lax.fori_loop(0, V // PAD, unpack, 0)
+
+    for d in range(1, NV):
+        t_copy(d).wait_send()
+    a_sibling().wait_send()
+    for cc in range(2):
+        for dy in (1, 3):
+            a_copy(dy, cc).wait_send()
+    for i in range(2):
+        f_copy(i).wait_send()
+    for n in range(NG):
+        for d in range(1, NX):
+            s_copy(n, d).wait_send()
+        if n >= 2:
+            left_z(n)
+        for way in range(2):
+            w3_copy(n, way).wait_send()
+            w3_forward(n, way).wait_send()
+    for part in range(4):
+        y_copy(part).wait_send()
+
+    def drain(j, carry):
+        for xx in range(2):
+            @pl.when(j > l)
+            def _():
+                hop(U, u_send, u_recv, j, xx, 1).wait_send()
+
+            @pl.when(j < l)
+            def _():
+                hop(D, d_send, d_recv, j, xx, -1).wait_send()
+
+        return carry
+
+    lax.fori_loop(0, O, drain, 0)
+
+
+def packed(amplitudes, w_ovvo, occ_irreps, vir_irreps):
+    smem = pl.BlockSpec(memory_space=pltpu.SMEM)
+    vmem = pl.BlockSpec(memory_space=pltpu.VMEM)
+    anym = pl.BlockSpec(memory_space=pl.ANY)
+    dma = pltpu.SemaphoreType.DMA
+    return pl.pallas_call(
+        packed_kernel,
+        out_shape=(jax.ShapeDtypeStruct((2, V, BV), BF), jax.ShapeDtypeStruct((1,), jnp.int32)),
+        in_specs=[smem, vmem, anym, anym],
+        out_specs=(vmem, smem),
+        scratch_shapes=[
+            pltpu.VMEM((NV, BV, BV), BF),
+            pltpu.VMEM((NX, NV, BV // NX, BV), BF),
+            pltpu.VMEM((O, NV, BV, BV), BF),
+            pltpu.VMEM((NV, V, BV), BF),
+            pltpu.VMEM((2, V, V), BF),
+            pltpu.VMEM((O * 2 * V, BV), F32),
+            pltpu.VMEM((O, 2, CAP, BV), BF),
+            pltpu.VMEM((O, 2, CAP, BV), BF),
+            pltpu.VMEM((O, 2, CAP, BV), BF),
+            pltpu.VMEM((2 * FR, BV), F32),
+            pltpu.VMEM((V, BV), jnp.int32),
+            pltpu.SMEM((O,), jnp.int32),
+            dma((7,)), dma((NV,)), dma((5,)), dma((NV,)), dma((2,)), dma((NG, 3)), dma((NG, 3)),
+            dma((NG, 8)), dma((NG, O)), dma((NG, 2)), dma((NG, 2)), dma((NG, 2)), dma((NG, 2)), dma((4,)), dma((4,)),
+            dma((O, 2)), dma((O, 2)), dma((O, 2)), dma((O, 2)),
+        ],
+        compiler_params=pltpu.CompilerParams(
+            collective_id=0, has_side_effects=True, vmem_limit_bytes=48 * 2**20
+        ),
+        name="packed_cycle",
+    )(occ_irreps, vir_irreps.reshape(V // BV, BV), amplitudes, w_ovvo)
+
+
+def shards(amplitudes, w_ovvo, occ_irreps, vir_irreps):
+    result, fits = packed(amplitudes, w_ovvo, occ_irreps, vir_irreps)
+    result = lax.cond(
+        fits[0] == 1,
+        lambda: result,
+        lambda: general(amplitudes, w_ovvo, occ_irreps, vir_irreps),
+    )
     return result[:, None]
 
 

time: 461 us -> 110 us (0.24)
  waiting for transfers between devices: 287 us -> 0 us
  Pallas kernels: 0 us -> 105 us
  blocking collectives: 87.5 us -> 0 us
  other arithmetic: 21.2 us -> 0 us
  starting transfers between devices: 20.9 us -> 0 us
  local copies, waits for them, and re-layouts: 22.1 us -> 2.74 us
  between operations: 15 us -> 0.71 us
  matrix products: 6.16 us -> 0 us
    ppermute x6 -> x0, waiting for transfers between devices: 249 us -> none  [swapped(): return lax.ppermute(block, axis, route)]
    pallas_call x0 -> x1, Pallas kernels: none -> 105 us  [packed(): pl.pallas_call(packed_kernel, out_shape=(jax.ShapeDtypeStruct((2, V, BV),...]
    all_to_all x2 -> x0, blocking collectives: 87.5 us -> none  [the longest x1 50.3 us: shards(): lax.all_to_all(own_tile[None], 'pair', split_axis=2, concat_axis=0, tiled...]
    unnamed x2 -> x0, waiting for transfers between devices: 37.5 us -> none
    ppermute x6 -> x0, starting transfers between devices: 20.9 us -> none  [swapped(): return lax.ppermute(block, axis, route)]
    unnamed x13 -> x2, local copies, waits for them, and re-layouts: 21.4 us -> 0.79 us
    select_n x5 -> x0, other arithmetic: 18.6 us -> none  [the longest x3 18.3 us: shards(): jnp.where(lower_half, jnp.concatenate([cycle_stack, partner], axis=0), jn...]
    dot_general x1 -> x0, matrix products: 6.16 us -> none  [shards(): jnp.einsum('kxac,kcb->xab', cycle_stack, weight_stack, preferred_element_...]
  transfers between devices with their start and end apart: 7 -> 0, of which waited for: 6 -> 0; matrix products, arithmetic and copies ran while one was open for 3% -> 0% of each run, Pallas kernels for 0% -> 0%
where the time goes in v2:
time: 110 us; the launch traced here: 109 us
  Pallas kernels  105 us (95%)
  local copies, waits for them, and re-layouts  2.74 us (2%)
    pallas_call x1, Pallas kernels, packed(): pl.pallas_call(packed_kernel, out_shape=(jax.ShapeDtypeStruct((2, V, BV),...  105 us

profile of v2, /device:TPU:6, one launch (start us, length us, event | category | flops | bytes accessed | tf_op | source)
XLA Modules:
  0.0 108.5 jit_solution(10766010768226706273)
XLA Ops:
  0.0 104.8 %packed_cycle.1 = (bf16[2,1024,128]{2,1,0:T(8,128)(2,1)}, s32[1]{0:T(128)}) custom-call(s32[8]{0:T(128)} %occ_ref.1, s32[8,128]{1,0:T(8,128)} %bitcast.43, bf16[2,1,1024,128]{3,2,1,0:T(8,128)(2,1)} %amp_ref.1, bf16[1,128,1024]{2,1,0:T(8,128)(2,1)} %w_ref.1), custom_call_target="tpu_custom_call" | custom-call | tf_op jit(solution)/shard_map/packed_cycle/pallas_call | solution.py:489
  105.5 2.2 %conditional.1 = (bf16[2,1,1024,128]{3,2,1,0:T(8,128)(2,1)S(1)}) conditional(s32[]{:T(128)} %bitcast.17, (s32[1024]{0:T(1024)}, s32[8]{0:T(128)}, bf16[2,1,1024,128]{3,2,1,0:T(8,128)(2,1)}, bf16[1,128,1024]{2,1,0:T(8,128)(2,1)}) %tuple.13, bf16[2,1024,128]{2,1,0:T(8,128)(2,1)} %get-tuple-element.26), branch_computations={%region_0.4_spmd, %region_4.5_spmd} | conditional | flops 4319346688 | bytes 91512152 | solution.py:520
  105.8 1.4 %copy.20 = bf16[2,1024,128]{1,0,2:T(2,128)(2,1)S(1)} copy(bf16[2,1024,128]{2,1,0:T(8,128)(2,1)} %param.1) | data formatting | bytes 1048576 | tf_op jit(solution)/shard_map/packed_cycle/pallas_call
  107.2 0.5 copy.24
  107.7 0.0 copy-start.2
  107.7 0.8 copy-done.2
Async XLA Ops:
  107.7 0.8 copy-start.2

commit v3 on v2

--- a/solution.py
+++ b/solution.py
@@ -86,13 +86,15 @@
 PAD = 32
 FR = CAP + 2 * PAD
 NG = 4
+NP = 2
+PR = CAP // NP
 GW = V // NG
 
 
 def packed_kernel(
     occ_ref, vir_ref, amp_ref, w_ref, out_ref, fits_ref,
-    T, S, W, R, cyc, C, Pk, U, D, Fin, key, st,
-    t_send, t_recv, a_send, a_recv, f_send, s_send, s_recv,
+    S, W, R, cyc, C, Pk, U, D, Fin, key, st,
+    a_send, a_recv, f_send, s_send, s_recv,
     w2_send, w2_recv, w3_send, w3_recv, w3f_send, w3f_recv, y_send, y_recv,
     u_send, u_recv, d_send, d_recv,
 ):
@@ -119,10 +121,8 @@
     def greet(p, q):
         pl.semaphore_signal(bar, inc=1, device_id=(p, q), device_id_type=MESH)
 
-    for d in range(1, NV):
-        greet(pair, (v + d) % NV)
-    for d in range(1, NX):
-        greet(at((x + d) % NX, z), v)
+    for d in range(1, NX * NV):
+        greet(at((x + d // NV) % NX, z), (v + d) % NV)
     for j in range(O):
         source = O * (l % 2) + j
 
@@ -140,19 +140,29 @@
 
     own_k = (l % 2 == half).astype(jnp.int32)
     ends = (l > 0).astype(jnp.int32) + (l < O - 1).astype(jnp.int32)
-    pl.semaphore_wait(bar, (NV - 1) + (NX - 1) + O - own_k + ends)
-
-    def w_piece(q):
-        return w_ref.at[0, :, pl.ds(pl.multiple_of(q * BV, BV), BV)]
-
-    def t_copy(d):
-        q = (v + d) % NV
-        return remote(w_piece(q), T.at[v], t_send.at[d - 1], t_recv.at[v], pair, q)
-
-    t_local = pltpu.make_async_copy(w_piece(v), T.at[v], t_recv.at[v])
-    t_local.start()
-    for d in range(1, NV):
-        t_copy(d).start()
+    pl.semaphore_wait(bar, NX * NV - 1 + O - own_k + ends)
+
+    XR = BV // NX
+
+    def chunk(n):
+        return (y + n) % NY
+
+    def blocks(n):
+        return pl.ds(2 * chunk(n), 2)
+
+    def quarter(q):
+        return pl.ds(pl.multiple_of(q * XR, XR), XR)
+
+    def s_copy(n, c, d):
+        p, q = (x + d) % NX, ((y - n + NY) % NY) * 2 + (core + c) % 2
+        src = w_ref.at[0, quarter(p), pl.ds(pl.multiple_of(q * BV, BV), BV)]
+        if n + c + d == 0:
+            return pltpu.make_async_copy(src, S.at[x, v], s_recv.at[x, v])
+        return remote(src, S.at[x, v], s_send.at[n, c, d], s_recv.at[x, v], at(p, z), q)
+
+    spread = [(n, c, d) for n in range(NG) for c in range(2) for d in range(NX)]
+    for which in spread:
+        s_copy(*which).start()
 
     a_local = pltpu.make_async_copy(amp_ref.at[core, 0], R.at[v], a_recv.at[v])
     a_local.start()
@@ -169,67 +179,46 @@
     def a_arrived(g):
         arrived(R.at[g], a_recv.at[g])
 
-    a_sibling().start()
-    for cc in range(2):
-        for dy in (1, 3):
-            a_copy(dy, cc).start()
-
-    XR = BV // NX
-
-    def chunk(n):
-        return (y + n) % NY
-
-    def blocks(n):
-        return pl.ds(2 * chunk(n), 2)
-
-    def quarter(q):
-        return pl.ds(pl.multiple_of(q * XR, XR), XR)
-
-    def s_copy(n, d):
-        q = (x + d) % NX
-        return remote(
-            T.at[blocks(n), quarter(q)], S.at[x, blocks(n)],
-            s_send.at[n, d - 1], s_recv.at[n, d - 1], at(q, z), v,
-        )
-
-    def spread_x(n):
-        for i in range(2):
-            g = 2 * chunk(n) + i
-            arrived(T.at[g], t_recv.at[g])
-        for d in range(1, NX):
-            s_copy(n, d).start()
-
-    def w2_copy(n, d, h):
-        q = (x - d + NX) % NX
-        src = T.at[blocks(n), quarter(x)] if d == 0 else S.at[q, blocks(n)]
-        dst = W.at[l, blocks(n), quarter(x)]
-        dz = 2 * q + half + O * h
-        return dz, src, dst, remote(src, dst, w2_send.at[n, 2 * d + h], w2_recv.at[n, l], at(x, dz), v)
+    odd = (half + l) % 2
+
+    def w2_copy(n, slot, way):
+        hops = 2 * slot + 2 - odd
+        step = (hops, -hops)[way]
+        q = ((l + step + O) % O) // 2
+        src, dst = S.at[q, blocks(n)], W.at[l, blocks(n), quarter(x)]
+        dz = (z + step + NZ) % NZ
+        return src, dst, remote(src, dst, w2_send.at[n, slot, way], w2_recv.at[n, l], at(x, dz), v)
 
     def move_z(n):
-        for d in range(NX):
-            if d:
-                q = (x - d + NX) % NX
-                arrived(S.at[q, blocks(n)], s_recv.at[n, d - 1])
-            for h in range(2):
-                dz, src, dst, copy = w2_copy(n, d, h)
-
-                @pl.when(dz != z)
+        for q in range(NX):
+            for c in range(2):
+                g = 2 * chunk(n) + c
+                arrived(S.at[q, g], s_recv.at[q, g])
+        for slot in (3, 2, 1, 0):
+            src, dst, up = w2_copy(n, slot, 0)
+            up.start()
+            src, dst, down = w2_copy(n, slot, 1)
+            if slot < 3:
+                down.start()
+            else:
+                @pl.when(odd == 1)
                 def _():
-                    copy.start()
-
-                @pl.when(dz == z)
+                    down.start()
+
+                @pl.when(odd == 0)
                 def _():
                     pltpu.make_async_copy(src, dst, w2_recv.at[n, l]).start()
 
     def left_z(n):
-        for d in range(NX):
-            for h in range(2):
-                dz, _, _, copy = w2_copy(n, d, h)
-
-                @pl.when(dz != z)
+        for slot in (3, 2, 1, 0):
+            w2_copy(n, slot, 0)[2].wait_send()
+            down = w2_copy(n, slot, 1)[2]
+            if slot < 3:
+                down.wait_send()
+            else:
+                @pl.when(odd == 1)
                 def _():
-                    copy.wait_send()
+                    down.wait_send()
 
     def w3_copy(n, way):
         block = W.at[:, blocks(n), quarter(x)]
@@ -332,22 +321,25 @@
 
         lax.fori_loop(0, 4, body, 0)
 
-    for n in range(NG):
-        spread_x(n)
     move_z(0)
+    a_sibling().start()
+    for cc in range(2):
+        for dy in (1, 3):
+            a_copy(dy, cc).start()
+    tables()
+    left_z(0)
     move_z(1)
-    tables()
     a_arrived(g_lo)
     f_copy(0).start()
     a_arrived(g_hi)
     f_copy(1).start()
-    left_z(0)
+    gather_x(0)
+    left_z(1)
     move_z(2)
-    gather_x(0)
     forward_x(0)
-    left_z(1)
+    gather_x(1)
+    left_z(2)
     move_z(3)
-    gather_x(1)
     a_arrived(v)
     a_arrived(sibling)
     a_arrived(g_lo + 1)
@@ -387,20 +379,25 @@
                     acc = jnp.where(colb == beta, C[pl.ds(start, CAP), :], acc)
                 Pk[j, xx] = acc.astype(BF)
 
-    def hop(buf, send, recv, j, xx, step):
-        return remote(buf.at[j, xx], buf.at[j, xx], send.at[j, xx], recv.at[j, xx], at(x, z + step), v)
-
-    def flow(buf, send, recv, j, xx, step, first):
+    def hop(buf, send, recv, j, c, step):
+        piece = buf.at[j, c // NP, pl.ds((c % NP) * PR, PR)]
+        return remote(piece, piece, send.at[j, c], recv.at[j, c], at(x, z + step), v)
+
+    def flow(buf, send, recv, j, c, step, first):
+        rows = pl.ds((c % NP) * PR, PR)
+
         @pl.when(first)
         def _():
-            buf[j, xx] = Pk[j, xx]
+            buf[j, c // NP, rows] = Pk[j, c // NP, rows]
 
         @pl.when(jnp.logical_not(first))
         def _():
-            hop(buf, send, recv, j, xx, step).wait_recv()
-            buf[j, xx] = (buf[j, xx].astype(F32) + Pk[j, xx].astype(F32)).astype(BF)
-
-        hop(buf, send, recv, j, xx, step).start()
+            hop(buf, send, recv, j, c, step).wait_recv()
+            buf[j, c // NP, rows] = (
+                buf[j, c // NP, rows].astype(F32) + Pk[j, c // NP, rows].astype(F32)
+            ).astype(BF)
+
+        hop(buf, send, recv, j, c, step).start()
 
     def tick(tau, carry):
         @pl.when(tau < 4)
@@ -408,14 +405,14 @@
             product(NG - 1, tau)
             pack(tau)
 
-        for xx in range(2):
+        for c in range(2 * NP):
             @pl.when(tau >= l)
             def _():
-                flow(U, u_send, u_recv, O - 1 + l - tau, xx, 1, l == 0)
+                flow(U, u_send, u_recv, O - 1 + l - tau, c, 1, l == 0)
 
             @pl.when(tau >= O - 1 - l)
             def _():
-                flow(D, d_send, d_recv, l - (O - 1 - tau), xx, -1, l == O - 1)
+                flow(D, d_send, d_recv, l - (O - 1 - tau), c, -1, l == O - 1)
 
         return carry
 
@@ -427,12 +424,14 @@
 
         @pl.when(l > 0)
         def _():
-            hop(U, u_send, u_recv, l, xx, 1).wait_recv()
+            for c in range(NP):
+                hop(U, u_send, u_recv, l, xx * NP + c, 1).wait_recv()
             Fin[mid, :] += U[l, xx].astype(F32)
 
         @pl.when(l < O - 1)
         def _():
-            hop(D, d_send, d_recv, l, xx, -1).wait_recv()
+            for c in range(NP):
+                hop(D, d_send, d_recv, l, xx * NP + c, -1).wait_recv()
             Fin[mid, :] += D[l, xx].astype(F32)
 
         def unpack(i, carry):
@@ -442,13 +441,13 @@
             for alpha in range(O):
                 first = jnp.clip(i * (PAD // 8) - st[alpha], -PAD // 8, CAP // 8) + PAD // 8
                 acc = jnp.where(held == alpha, Fin[pl.ds(first * 8 + xx * FR, PAD), :], acc)
-            out_ref[xx, rows, :] = acc.astype(BF)
+            out_ref[xx, 0, rows, :] = acc.astype(BF)
             return carry
 
         lax.fori_loop(0, V // PAD, unpack, 0)
 
-    for d in range(1, NV):
-        t_copy(d).wait_send()
+    for which in spread[1:]:
+        s_copy(*which).wait_send()
     a_sibling().wait_send()
     for cc in range(2):
         for dy in (1, 3):
@@ -456,9 +455,7 @@
     for i in range(2):
         f_copy(i).wait_send()
     for n in range(NG):
-        for d in range(1, NX):
-            s_copy(n, d).wait_send()
-        if n >= 2:
+        if n == NG - 1:
             left_z(n)
         for way in range(2):
             w3_copy(n, way).wait_send()
@@ -467,14 +464,14 @@
         y_copy(part).wait_send()
 
     def drain(j, carry):
-        for xx in range(2):
+        for c in range(2 * NP):
             @pl.when(j > l)
             def _():
-                hop(U, u_send, u_recv, j, xx, 1).wait_send()
+                hop(U, u_send, u_recv, j, c, 1).wait_send()
 
             @pl.when(j < l)
             def _():
-                hop(D, d_send, d_recv, j, xx, -1).wait_send()
+                hop(D, d_send, d_recv, j, c, -1).wait_send()
 
         return carry
 
@@ -488,11 +485,10 @@
     dma = pltpu.SemaphoreType.DMA
     return pl.pallas_call(
         packed_kernel,
-        out_shape=(jax.ShapeDtypeStruct((2, V, BV), BF), jax.ShapeDtypeStruct((1,), jnp.int32)),
+        out_shape=(jax.ShapeDtypeStruct((2, 1, V, BV), BF), jax.ShapeDtypeStruct((1,), jnp.int32)),
         in_specs=[smem, vmem, anym, anym],
         out_specs=(vmem, smem),
         scratch_shapes=[
-            pltpu.VMEM((NV, BV, BV), BF),
             pltpu.VMEM((NX, NV, BV // NX, BV), BF),
             pltpu.VMEM((O, NV, BV, BV), BF),
             pltpu.VMEM((NV, V, BV), BF),
@@ -504,9 +500,9 @@
             pltpu.VMEM((2 * FR, BV), F32),
             pltpu.VMEM((V, BV), jnp.int32),
             pltpu.SMEM((O,), jnp.int32),
-            dma((7,)), dma((NV,)), dma((5,)), dma((NV,)), dma((2,)), dma((NG, 3)), dma((NG, 3)),
-            dma((NG, 8)), dma((NG, O)), dma((NG, 2)), dma((NG, 2)), dma((NG, 2)), dma((NG, 2)), dma((4,)), dma((4,)),
-            dma((O, 2)), dma((O, 2)), dma((O, 2)), dma((O, 2)),
+            dma((5,)), dma((NV,)), dma((2,)), dma((NG, 2, NX)), dma((NX, NV)),
+            dma((NG, 4, 2)), dma((NG, O)), dma((NG, 2)), dma((NG, 2)), dma((NG, 2)), dma((NG, 2)), dma((4,)), dma((4,)),
+            dma((O, 2 * NP)), dma((O, 2 * NP)), dma((O, 2 * NP)), dma((O, 2 * NP)),
         ],
         compiler_params=pltpu.CompilerParams(
             collective_id=0, has_side_effects=True, vmem_limit_bytes=48 * 2**20
@@ -517,12 +513,11 @@
 
 def shards(amplitudes, w_ovvo, occ_irreps, vir_irreps):
     result, fits = packed(amplitudes, w_ovvo, occ_irreps, vir_irreps)
-    result = lax.cond(
+    return lax.cond(
         fits[0] == 1,
         lambda: result,
-        lambda: general(amplitudes, w_ovvo, occ_irreps, vir_irreps),
+        lambda: general(amplitudes, w_ovvo, occ_irreps, vir_irreps)[:, None],
     )
-    return result[:, None]
 
 
 def solution(mesh):

time: 110 us -> 103 us (0.936)
  Pallas kernels: 105 us -> 99.6 us
    pallas_call x1, Pallas kernels: 105 us -> 99.6 us  [packed(): pl.pallas_call(packed_kernel, out_shape=(jax.ShapeDtypeStruct((2, 1, V, B...]
    pallas_call x1 -> x0, local copies, waits for them, and re-layouts: 1.41 us -> none
where the time goes in v3:
time: 103 us; the launch traced here: 102 us
  Pallas kernels  99.6 us (97%)
  local copies, waits for them, and re-layouts  1.87 us (2%)
    pallas_call x1, Pallas kernels, packed(): pl.pallas_call(packed_kernel, out_shape=(jax.ShapeDtypeStruct((2, 1, V, B...  99.6 us

profile of v3, /device:TPU:6, one launch (start us, length us, event | category | flops | bytes accessed | tf_op | source)
XLA Modules:
  0.0 102.3 jit_solution(7017283463790403238)
XLA Ops:
  0.0 99.6 %packed_cycle.1 = (bf16[2,1,1024,128]{3,2,1,0:T(8,128)(2,1)}, s32[1]{0:T(128)}) custom-call(s32[8]{0:T(128)} %occ_ref.1, s32[8,128]{1,0:T(8,128)} %bitcast.41, bf16[2,1,1024,128]{3,2,1,0:T(8,128)(2,1)} %amp_ref.1, bf16[1,128,1024]{2,1,0:T(8,128)(2,1)} %w_ref.1), custom_call_target="tpu_custom_call" | custom-call | tf_op jit(solution)/shard_map/packed_cycle/pallas_call | solution.py:486
  100.2 0.2 conditional.1
  100.5 1.9 %copy.36 = bf16[2,1,1024,128]{3,2,1,0:T(8,128)(2,1)} copy(bf16[2,1,1024,128]{3,2,1,0:T(8,128)(2,1)} %get-tuple-element.38) | data formatting | bytes 1048576

commit v4 on v3

--- a/solution.py
+++ b/solution.py
@@ -17,7 +17,7 @@
 NV = 8
 V = 1024
 BV = 128
-CAP = 288
+CAP = 272
 
 
 def swapped(block, axis, stride):
@@ -86,8 +86,8 @@
 PAD = 32
 FR = CAP + 2 * PAD
 NG = 4
-NP = 2
-PR = CAP // NP
+PIECES = ((0, 144), (144, 128))
+NP = len(PIECES)
 GW = V // NG
 
 
@@ -95,7 +95,7 @@
     occ_ref, vir_ref, amp_ref, w_ref, out_ref, fits_ref,
     S, W, R, cyc, C, Pk, U, D, Fin, key, st,
     a_send, a_recv, f_send, s_send, s_recv,
-    w2_send, w2_recv, w3_send, w3_recv, w3f_send, w3f_recv, y_send, y_recv,
+    w2_send, w2_recv, p_send, p_recv, pf_send, pf_recv, w3_send, w3_recv, w3f_send, w3f_recv, y_send, y_recv,
     u_send, u_recv, d_send, d_recv,
 ):
     pair, v = lax.axis_index("pair"), lax.axis_index("virt")
@@ -234,6 +234,32 @@
         block = W.at[pl.ds(4 * way, 4), blocks(n), quarter((x + (3, 1)[way]) % NX)]
         return remote(block, block, w3f_send.at[n, way], w3f_recv.at[n, way], at((x + (1, 3)[way]) % NX, z), v)
 
+    LAST = NG - 1
+
+    def pair_copy(j, way):
+        block = W.at[j, blocks(LAST), quarter(x)]
+        return remote(block, block, p_send.at[j, way], p_recv.at[j, way], at((x + (1, 3)[way]) % NX, z), v)
+
+    def pair_forward(j, way):
+        block = W.at[j, blocks(LAST), quarter((x + (3, 1)[way]) % NX)]
+        return remote(block, block, pf_send.at[j], pf_recv.at[j], at((x + (1, 3)[way]) % NX, z), v)
+
+    def gather_pair(s):
+        for j in (s, O - 1 - s):
+            arrived(W.at[j, blocks(LAST), quarter(x)], w2_recv.at[LAST, j])
+            for way in range(2):
+                pair_copy(j, way).start()
+
+    def forward_pair(s):
+        for way, j in enumerate((s, O - 1 - s)):
+            arrived(W.at[j, blocks(LAST), quarter((x + (3, 1)[way]) % NX)], p_recv.at[j, way])
+            pair_forward(j, way).start()
+
+    def gathered_pair(s):
+        for way, j in enumerate((s, O - 1 - s)):
+            arrived(W.at[j, blocks(LAST), quarter((x + (1, 3)[way]) % NX)], p_recv.at[j, 1 - way])
+            arrived(W.at[j, blocks(LAST), quarter((x + 2) % NX)], pf_recv.at[j])
+
     def forward_x(n):
         for way in range(2):
             arrived(W.at[:, blocks(n), quarter((x + (3, 1)[way]) % NX)], w3_recv.at[n, way])
@@ -250,21 +276,30 @@
         g, dy = ((g_lo, 1), (g_hi, 3))[i]
         return remote(R.at[g], R.at[g], f_send.at[i], a_recv.at[g], pair, ((y + dy) % NY) * 2 + core)
 
-    def cycle_part(part):
+    def place(e, i):
+        return ((y + e) % NY) * 2 + i
+
+    FIRST = [(e, i) for e in (0, 1, 3) for i in range(2)]
+    LATE = [(2, i) for i in range(2)]
+
+    def cycle_rows(r, columns):
+        row = pl.ds(pl.multiple_of(r * BV, BV), BV)
+        for which in columns:
+            q = place(*which)
+            column = pl.ds(pl.multiple_of(q * BV, BV), BV)
+            other = R[r, column, :].astype(F32)
+            cyc[core, row, column] = (2.0 * R[q, row, :].astype(F32) - other.T).astype(BF)
+
+    def cycle_chip(e, columns):
         def body(i, carry):
-            r = part * 2 + i
-            row = pl.ds(pl.multiple_of(r * BV, BV), BV)
-            for q in range(NV):
-                mine = R[q, row, :].astype(F32)
-                other = R[r, q * BV:(q + 1) * BV, :].astype(F32)
-                cyc[core, row, q * BV:(q + 1) * BV] = (2.0 * mine - other.T).astype(BF)
+            cycle_rows(place(e, i), columns)
             return carry
 
         lax.fori_loop(0, 2, body, 0)
-        y_copy(part).start()
-
-    def y_copy(part):
-        rows = pl.ds(part * 256, 256)
+
+    def y_copy(e):
+        part = (y + e) % NY
+        rows = pl.ds(pl.multiple_of(part * 256, 256), 256)
         return remote(
             cyc.at[core, rows], cyc.at[core, rows], y_send.at[part], y_recv.at[part], pair, sibling
         )
@@ -293,39 +328,33 @@
 
         lax.fori_loop(0, V // BV, body, 0)
 
-    def product(n, s):
-        g = chunk(n)
-        weights = jnp.concatenate(
-            [W[O - 1 - s, blocks(n)].reshape(GW, BV), W[s, blocks(n)].reshape(GW, BV)], axis=1
-        )
-        columns = pl.ds(pl.multiple_of(g * GW, GW), GW)
+    def product(chunks, s, first):
+        weights = jnp.concatenate([
+            jnp.concatenate([W[j, blocks(n)].reshape(2 * BV, BV) for n in chunks], axis=0)
+            for j in (O - 1 - s, s)
+        ], axis=1)
 
         def body(xx, carry):
             for m in range(4):
-                value = jnp.dot(
-                    cyc[xx, pl.ds(m * 256, 256), columns], weights, preferred_element_type=F32
-                )
+                rows = pl.ds(m * 256, 256)
+                left = jnp.concatenate([
+                    cyc[xx, rows, pl.ds(pl.multiple_of(chunk(n) * 256, 256), 256)] for n in chunks
+                ], axis=1)
+                value = jnp.dot(left, weights, preferred_element_type=F32)
                 for side in range(2):
                     j = (O - 1 - s, s)[side]
                     rows = pl.ds(pl.multiple_of((j * 2 + xx) * V + m * 256, 256), 256)
                     part = value[:, side * BV:(side + 1) * BV]
-                    C[rows, :] = part if n == 0 else C[rows, :] + part
+                    C[rows, :] = part if first else C[rows, :] + part
             return carry
 
         lax.fori_loop(0, 2, body, 0)
 
-    def products(n):
-        def body(s, carry):
-            product(n, s)
-            return carry
-
-        lax.fori_loop(0, 4, body, 0)
-
-    move_z(0)
     a_sibling().start()
     for cc in range(2):
         for dy in (1, 3):
             a_copy(dy, cc).start()
+    move_z(0)
     tables()
     left_z(0)
     move_z(1)
@@ -344,26 +373,30 @@
     a_arrived(sibling)
     a_arrived(g_lo + 1)
     a_arrived(g_hi - 1)
+    for e in (0, 1, 3):
+        cycle_chip(e, FIRST)
+    forward_x(1)
     a_arrived(((y + 2) % NY) * 2)
     a_arrived(((y + 2) % NY) * 2 + 1)
-    cycle_part(0)
-    cycle_part(1)
-    forward_x(1)
+    for e in (0, 1, 3):
+        cycle_chip(e, LATE)
+        y_copy(e).start()
     gather_x(2)
-    cycle_part(2)
-    cycle_part(3)
+    cycle_chip(2, FIRST + LATE)
+    y_copy(2).start()
     forward_x(2)
     gathered_x(0)
     for part in range(4):
         arrived(cyc.at[1 - core, pl.ds(part * 256, 256)], y_recv.at[part])
-    products(0)
-    gather_x(3)
+    for s in range(4):
+        gather_pair(s)
     gathered_x(1)
-    products(1)
-    forward_x(3)
     gathered_x(2)
-    products(2)
-    gathered_x(3)
+    for s in range(4):
+        product((0, 1, 2), s, True)
+        if s == 1:
+            for r in range(4):
+                forward_pair(r)
 
     colb = jnp.broadcast_to(vir_ref[pl.ds(v, 1), :], (CAP, BV))
     occ_left = occ_ref[pair // O]
@@ -380,11 +413,11 @@
                 Pk[j, xx] = acc.astype(BF)
 
     def hop(buf, send, recv, j, c, step):
-        piece = buf.at[j, c // NP, pl.ds((c % NP) * PR, PR)]
+        piece = buf.at[j, c // NP, pl.ds(*PIECES[c % NP])]
         return remote(piece, piece, send.at[j, c], recv.at[j, c], at(x, z + step), v)
 
     def flow(buf, send, recv, j, c, step, first):
-        rows = pl.ds((c % NP) * PR, PR)
+        rows = pl.ds(*PIECES[c % NP])
 
         @pl.when(first)
         def _():
@@ -400,9 +433,9 @@
         hop(buf, send, recv, j, c, step).start()
 
     def tick(tau, carry):
-        @pl.when(tau < 4)
-        def _():
-            product(NG - 1, tau)
+        if isinstance(tau, int):
+            gathered_pair(tau)
+            product((LAST,), tau, False)
             pack(tau)
 
         for c in range(2 * NP):
@@ -416,7 +449,9 @@
 
         return carry
 
-    lax.fori_loop(0, O - 1, tick, 0)
+    for tau in range(4):
+        tick(tau, 0)
+    lax.fori_loop(4, O - 1, tick, 0)
 
     for xx in range(2):
         mid = pl.ds(xx * FR + PAD, CAP)
@@ -457,9 +492,13 @@
     for n in range(NG):
         if n == NG - 1:
             left_z(n)
-        for way in range(2):
+        for way in range(2) if n < LAST else ():
             w3_copy(n, way).wait_send()
             w3_forward(n, way).wait_send()
+    for j in range(O):
+        for way in range(2):
+            pair_copy(j, way).wait_send()
+        pair_forward(j, j // 4).wait_send()
     for part in range(4):
         y_copy(part).wait_send()
 
@@ -501,7 +540,7 @@
             pltpu.VMEM((V, BV), jnp.int32),
             pltpu.SMEM((O,), jnp.int32),
             dma((5,)), dma((NV,)), dma((2,)), dma((NG, 2, NX)), dma((NX, NV)),
-            dma((NG, 4, 2)), dma((NG, O)), dma((NG, 2)), dma((NG, 2)), dma((NG, 2)), dma((NG, 2)), dma((4,)), dma((4,)),
+            dma((NG, 4, 2)), dma((NG, O)), dma((O, 2)), dma((O, 2)), dma((O,)), dma((O,)), dma((NG, 2)), dma((NG, 2)), dma((NG, 2)), dma((NG, 2)), dma((4,)), dma((4,)),
             dma((O, 2 * NP)), dma((O, 2 * NP)), dma((O, 2 * NP)), dma((O, 2 * NP)),
         ],
         compiler_params=pltpu.CompilerParams(

time: 103 us -> 100 us (0.971)
  Pallas kernels: 99.6 us -> 96.5 us
    pallas_call x1, Pallas kernels: 99.6 us -> 96.5 us  [packed(): pl.pallas_call(packed_kernel, out_shape=(jax.ShapeDtypeStruct((2, 1, V, B...]
where the time goes in v4:
time: 100 us; the launch traced here: 99.2 us
  Pallas kernels  96.5 us (96%)
  local copies, waits for them, and re-layouts  1.87 us (2%)
    pallas_call x1, Pallas kernels, packed(): pl.pallas_call(packed_kernel, out_shape=(jax.ShapeDtypeStruct((2, 1, V, B...  96.5 us

profile of v4, /device:TPU:6, one launch (start us, length us, event | category | flops | bytes accessed | tf_op | source)
XLA Modules:
  0.0 99.2 jit_solution(15966165191016161135)
XLA Ops:
  0.0 96.5 %packed_cycle.1 = (bf16[2,1,1024,128]{3,2,1,0:T(8,128)(2,1)}, s32[1]{0:T(128)}) custom-call(s32[8]{0:T(128)} %occ_ref.1, s32[8,128]{1,0:T(8,128)} %bitcast.41, bf16[2,1,1024,128]{3,2,1,0:T(8,128)(2,1)} %amp_ref.1, bf16[1,128,1024]{2,1,0:T(8,128)(2,1)} %w_ref.1), custom_call_target="tpu_custom_call" | custom-call | tf_op jit(solution)/shard_map/packed_cycle/pallas_call | solution.py:525
  97.1 0.2 conditional.1
  97.3 1.9 %copy.36 = bf16[2,1,1024,128]{3,2,1,0:T(8,128)(2,1)} copy(bf16[2,1,1024,128]{3,2,1,0:T(8,128)(2,1)} %get-tuple-element.38) | data formatting | bytes 1048576

commit v5 on v4

--- a/solution.py
+++ b/solution.py
@@ -392,11 +392,10 @@
         gather_pair(s)
     gathered_x(1)
     gathered_x(2)
+    product((0, 1, 2), 0, True)
     for s in range(4):
-        product((0, 1, 2), s, True)
-        if s == 1:
-            for r in range(4):
-                forward_pair(r)
+        forward_pair(s)
+    product((0, 1, 2), 1, True)
 
     colb = jnp.broadcast_to(vir_ref[pl.ds(v, 1), :], (CAP, BV))
     occ_left = occ_ref[pair // O]
@@ -451,6 +450,8 @@
 
     for tau in range(4):
         tick(tau, 0)
+        if tau < 2:
+            product((0, 1, 2), tau + 2, True)
     lax.fori_loop(4, O - 1, tick, 0)
 
     for xx in range(2):

time: 100 us -> 99.9 us (level)
  no operation moved by 1% of the time
where the time goes in v5:
time: 99.9 us; the launch traced here: 98.3 us
  Pallas kernels  95.6 us (96%)
  local copies, waits for them, and re-layouts  1.87 us (2%)
    pallas_call x1, Pallas kernels, packed(): pl.pallas_call(packed_kernel, out_shape=(jax.ShapeDtypeStruct((2, 1, V, B...  95.6 us

profile of v5, /device:TPU:6, one launch (start us, length us, event | category | flops | bytes accessed | tf_op | source)
XLA Modules:
  0.0 98.3 jit_solution(16447446261627112176)
XLA Ops:
  0.0 95.6 %packed_cycle.1 = (bf16[2,1,1024,128]{3,2,1,0:T(8,128)(2,1)}, s32[1]{0:T(128)}) custom-call(s32[8]{0:T(128)} %occ_ref.1, s32[8,128]{1,0:T(8,128)} %bitcast.41, bf16[2,1,1024,128]{3,2,1,0:T(8,128)(2,1)} %amp_ref.1, bf16[1,128,1024]{2,1,0:T(8,128)(2,1)} %w_ref.1), custom_call_target="tpu_custom_call" | custom-call | tf_op jit(solution)/shard_map/packed_cycle/pallas_call | solution.py:526
  96.1 0.2 conditional.1
  96.4 1.9 %copy.36 = bf16[2,1,1024,128]{3,2,1,0:T(8,128)(2,1)} copy(bf16[2,1,1024,128]{3,2,1,0:T(8,128)(2,1)} %get-tuple-element.38) | data formatting | bytes 1048576
